TPU v7x, 32 devices: a whole 2x2x4 slice. The times are simulated.
32 devices in a mesh: groups: 2 (over y), col: 16 (over z, x, core).
Axes of the slice: x: 2, y: 2, z: 4, core: 2. Of those that a mesh axis runs over, the one named last changes fastest.
Arguments:
- cooccur_slab: bfloat16 [4096, 32768], P('groups', 'col'), parts along dimension 0, may hold values from 0 to 0.4861359, as said below
- test_matrix: bfloat16 [32768, 256], P('col'), may hold values from -0.03125 to 0.03125
Outputs:
- projection: float32 [512, 32768], P('groups', 'col'), parts along dimension 0
There are 2 independent parts, one for each index of `groups`. A program takes and returns all parts, laid end to end along the dimension named above; an argument that names none is the same for every part. Nothing has to cross between parts.
Inputs may be any that keep to these rules, and one draw needn't show every extreme that they name: `cooccur_slab`: entries are non-negative, as in a positive PMI matrix.
All inputs are finite; a program needn't handle non-finite values.
Results may differ from a plain program's by a relative error of at most 0.0018.
Values may be sent and summed in bfloat16 or wider, within the bound.
A program may use at most 64 MiB of HBM per device.

v0:
```python
import jax
import jax.numpy as jnp
from jax import lax
from jax.sharding import PartitionSpec as P


def orthonormal(sketch_part, gram_matrix):
    lower_factor = jnp.linalg.cholesky(gram_matrix)
    solved = jax.scipy.linalg.solve_triangular(lower_factor, sketch_part.T, lower=True)
    return solved.T.astype(jnp.bfloat16)


def contract_rows(left, right):
    return lax.dot_general(
        left, right, (((0,), (0,)), ((), ())), preferred_element_type=jnp.float32
    )


def contract_rows_exact(left, right):
    return lax.dot_general(
        left,
        right,
        (((0,), (0,)), ((), ())),
        precision=lax.Precision.HIGHEST,
        preferred_element_type=jnp.float32,
    )


def local(cooccur_slab, test_matrix):
    partial_sketch = jnp.dot(cooccur_slab, test_matrix, preferred_element_type=jnp.float32)
    sketch = lax.psum(partial_sketch, "col")
    gram_matrix = contract_rows_exact(sketch, sketch)
    orthobasis = orthonormal(sketch, gram_matrix)
    projection = contract_rows(orthobasis, cooccur_slab)
    return projection


def solution(mesh):
    return jax.shard_map(
        local,
        mesh=mesh,
        in_specs=(P("groups", "col"), P("col", None)),
        out_specs=P("groups", "col"),
        check_vma=False,
    )
```

profile of v0, /device:TPU:0, one launch (start us, length us, event | category | flops | bytes accessed | tf_op | source)
XLA Modules:
  0.0 205.9 jit_solution(15757746622125951024)
XLA Ops:
  6.5 1.2 copy-done
  7.8 7.1 %fusion.14 = f32[2048,256]{1,0:T(8,128)} fusion(bf16[2048,2048]{1,0:T(8,128)(2,1)} %param.2, bf16[2048,256]{1,0:T(8,128)(2,1)S(1)} %copy-done), kind=kOutput, calls=%fused_computation.34 | convolution fusion | flops 2147483648 | bytes 11534336 | tf_op jit(solution)/shard_map/dot_general | solution.py:30
  14.9 100.5 %all-reduce.3.cloned.1.call-done = f32[2048,256]{1,0:T(8,128)} async-done(((f32[2048,256]{1,0:T(8,128)}), f32[2048,256]{1,0:T(8,128)}) %all-reduce.3.cloned.1.call-update) | async-done | bytes 2097168 | tf_op jit(solution)/shard_map/psum | solution.py:31
  115.4 5.7 %fusion.15 = f32[256,256]{1,0:T(8,128)S(1)} fusion(f32[2048,256]{1,0:T(8,128)} %all-reduce.3.cloned.1.call-done), kind=kOutput, calls=%fused_computation.35 | convolution fusion | flops 1610612736 | bytes 2359296 | tf_op jit(solution)/shard_map/dot_general | solution.py:20
  121.1 0.8 copy.3
  121.9 1.0 fusion.6
  122.9 0.7 copy-done.3
  123.6 11.7 %cholesky.50 = f32[128,128]{1,0:T(8,128)S(1)} custom-call(f32[128,128]{1,0:T(8,128)S(1)} %cholesky.118), custom_call_target="Cholesky" | custom-call | tf_op jit(solution)/shard_map/jit(cholesky)/cholesky | solution.py:8
  135.4 9.8 %custom-call.15 = f32[1,128,128]{1,2,0:T(8,128)S(1)} custom-call(f32[1,128,128]{2,1,0:T(8,128)S(1)} %get-tuple-element.26), custom_call_target="InvertDiagBlocksLowerTriangular" | custom-call | tf_op jit(solution)/shard_map/jit(cholesky)/cholesky | solution.py:8
  145.2 1.0 constant_dynamic-update-slice_fusion.1
  146.3 1.3 convolution_subtract_fusion.1
  147.6 11.7 %cholesky.105 = f32[128,128]{1,0:T(8,128)S(1)} custom-call(f32[128,128]{1,0:T(8,128)S(1)} %convolution_subtract_fusion.1), custom_call_target="Cholesky" | custom-call | tf_op jit(solution)/shard_map/jit(cholesky)/cholesky | solution.py:8
  159.3 0.7 compare_reduce_fusion
  161.3 1.0 select_select_fusion
  162.3 5.2 %while.1 = (s32[]{:T(128)}, f32[256,256]{1,0:T(8,128)S(1)}, s32[2,2]{1,0:T(2,128)S(1)}, f32[2,128,128]{2,1,0:T(8,128)}, s32[]{:T(128)}) while((s32[]{:T(128)}, f32[256,256]{1,0:T(8,128)S(1)}, s32[2,2]{1,0:T(2,128)S(1)}, f32[2,128,128]{2,1,0:T(8,128)}, s32[]{:T(128)}) %tuple.24), condition=%wide.while_cond, body=%wide.while_body.sunk | while | flops 2 | bytes 132205 | solution.py:9
  162.3 0.6 fusion.26
  162.9 2.0 bitcast_dynamic-update-slice_fusion.2
  164.9 0.6 fusion.26
  165.5 2.0 bitcast_dynamic-update-slice_fusion.2
  167.5 20.5 %custom-call.16 = f32[2,128,128]{1,2,0:T(8,128)S(1)} custom-call(f32[2,128,128]{2,1,0:T(8,128)} %get-tuple-element.12), custom_call_target="InvertDiagBlocksLowerTriangular" | custom-call | tf_op jit(solution)/shard_map/jit(_solve_triangular)/triangular_solve | solution.py:9
  188.0 1.1 fusion.13
  189.1 1.8 convolution_subtract_fusion
  190.9 1.1 convolution_convert_fusion
  192.0 7.1 %fusion.2 = f32[256,2048]{1,0:T(8,128)} fusion(bf16[2048,2048]{1,0:T(8,128)(2,1)} %param.2, bf16[128,2048]{1,0:T(8,128)(2,1)S(1)} %convolution_convert_fusion, bf16[128,2048]{1,0:T(8,128)(2,1)S(1)} %get-tuple-element.29), kind=kOutput, calls=%fused_computation.7 | convolution fusion | flops 2149580800 | bytes 11534336 | tf_op jit(solution)/shard_map/dot_general | solution.py:14
  (17 shorter events, 0.2 us)
Async XLA Ops:
  6.5 1.2 copy-start
  6.5 108.9 %all-reduce.3.cloned.1.call-start = ((), (), s32[]{:S(2)}) async-start(), calls=%async_computation | async-start | bytes 4194304 | tf_op jit(solution)/shard_map/psum | solution.py:31
  121.1 66.9 %copy-start.1 = (f32[2048,256]{1,0:T(8,128)S(1)}, f32[2048,256]{1,0:T(8,128)}, u32[]{:S(2)}) copy-start(f32[2048,256]{1,0:T(8,128)} %all-reduce.3.cloned.1.call-done) | copy-start | bytes 6291460
  122.9 0.7 copy-start.3
  159.3 2.0 copy-start.2
Sparse Core Ops, SparseCore 0:
  15.0 100.4 all-reduce.2
where the time goes:
time: 206 us
  waiting for transfers between devices  101 us (49%)
  other arithmetic  56.5 us (27%)
  matrix products  26.1 us (13%)
  between operations  14.8 us (7%)
  local copies, waits for them, and re-layouts  8.03 us (4%)
    psum x1, waiting for transfers between devices, local(): sketch = lax.psum(partial_sketch, 'col')  101 us
    another operation x6, other arithmetic, orthonormal(): lower_factor = jnp.linalg.cholesky(gram_matrix)  34 us
    another operation x3, other arithmetic, orthonormal(): jax.scipy.linalg.solve_triangular(lower_factor, sketch_part.T, lower=True)  21.5 us
    dot_general x1, matrix products, contract_rows(): lax.dot_general(left, right, (((0,), (0,)), ((), ())), preferred_element_...  7.06 us
    dot_general x1, matrix products, local(): jnp.dot(cooccur_slab, test_matrix, preferred_element_type=jnp.float32)  7.05 us
    dot_general x1, matrix products, contract_rows_exact(): lax.dot_general(left, right, (((0,), (0,)), ((), ())), precision=lax.Prec...  5.68 us
    another operation x6, local copies, waits for them, and re-layouts  5.17 us
  transfers between devices with their start and end apart: 1, of which 1 were waited for; matrix products, arithmetic and copies ran while one was open for 0% of the time, Pallas kernels for 0%

commit v1 on v0

v1 whole, which is shorter than its diff:
```python
import functools

import jax
import jax.numpy as jnp
from jax import lax
from jax.experimental import pallas as pl
from jax.experimental.pallas import tpu as pltpu
from jax.sharding import PartitionSpec as P

F32 = jnp.float32
BF16 = jnp.bfloat16
MESH = pl.DeviceIdType.MESH
HIGHEST = lax.Precision.HIGHEST


def sketch_kernel(
    nx, nz, nch, slab_hbm, test_hbm, gram_ref, cross_ref,
    slab, test, part, core_in, half, x_in, quarter, z_in, sketch, split,
    load_sem, core_sem, x_sem, z_sem, gz_sem, gx_sem, gc_sem,
):
    ncol = 2 * nx * nz
    rows, width = slab.shape
    k = test.shape[1]
    rc = rows // nch
    hr, xr, own = rc // 2, rc // (2 * nx), rc // ncol
    me = lax.axis_index("col")
    c = lax.rem(me, 2)
    x = lax.rem(me // 2, nx)
    z = me // (2 * nx)

    def device(z_, x_, c_):
        return {"col": (z_ * nx + x_) * 2 + c_}

    core_peer = device(z, x, 1 - c)
    x_peers = [lax.rem(x + d, nx) for d in range(1, nx)]
    z_peers = [lax.rem(z + d, nz) for d in range(1, nz)]

    load_test = pltpu.make_async_copy(test_hbm, test, load_sem.at[nch])
    load_test.start()
    loads = []
    for q in range(nch):
        at = pl.ds(q * rc, rc)
        load = pltpu.make_async_copy(slab_hbm.at[at], slab.at[at], load_sem.at[q])
        load.start()
        loads.append(load)

    barrier = pltpu.get_barrier_semaphore()
    peers = [core_peer] + [device(z, p, c) for p in x_peers] + [device(p, x, c) for p in z_peers]
    for peer in peers:
        pl.semaphore_signal(barrier, inc=1, device_id=peer, device_id_type=MESH)

    def remote(src, dst, sems, index, peer):
        return pltpu.make_async_remote_copy(
            src_ref=src, dst_ref=dst,
            send_sem=sems.at[(0,) + index], recv_sem=sems.at[(1,) + index],
            device_id=peer, device_id_type=MESH,
        )

    sent = []
    flights = {}

    def start(name, q, copies):
        for copy in copies:
            copy.start()
        sent.extend(copies)
        flights[name, q] = copies

    def arrive(name, q):
        for copy in flights[name, q]:
            copy.wait_recv()

    def rows_at(first, size):
        return pl.ds(pl.multiple_of(first, 8), size)

    def stage_compute(q):
        if q == 0:
            load_test.wait()
        loads[q].wait()
        tile = 128

        @pl.loop(0, rc // tile)
        def _(i):
            at = rows_at(q * rc + i * tile, tile)
            part[at, :] = jnp.dot(slab[at, :], test[...], preferred_element_type=F32)

        if q == 0:
            pl.semaphore_wait(barrier, len(peers))
        src = part.at[rows_at(q * rc + (1 - c) * hr, hr)]
        start("core", q, [remote(src, core_in.at[q], core_sem, (q,), core_peer)])

    def stage_core(q):
        arrive("core", q)
        half[q] = part[rows_at(q * rc + c * hr, hr), :] + core_in[q]
        start("x", q, [
            remote(half.at[q, rows_at(p * xr, xr)], x_in.at[q, d], x_sem, (q, d), device(z, p, c))
            for d, p in enumerate(x_peers)
        ])

    def stage_x(q):
        arrive("x", q)
        total = half[q, rows_at(x * xr, xr), :]
        for d in range(nx - 1):
            total = total + x_in[q, d]
        quarter[q] = total
        start("z", q, [
            remote(quarter.at[q, rows_at(p * own, own)], z_in.at[q, d], z_sem, (q, d), device(p, x, c))
            for d, p in enumerate(z_peers)
        ])

    def stage_z(q):
        arrive("z", q)
        total = quarter[q, rows_at(z * own, own), :]
        for d in range(nz - 1):
            total = total + z_in[q, d]
        at = rows_at(q * rc + c * hr + x * xr + z * own, own)
        sketch[at, :] = total
        start("gz", q, [
            remote(sketch.at[at], sketch.at[at], gz_sem, (q, d), device(p, x, c))
            for d, p in enumerate(z_peers)
        ])

    def stage_gz(q):
        arrive("gz", q)
        at = rows_at(q * rc + c * hr + x * xr, xr)
        start("gx", q, [
            remote(sketch.at[at], sketch.at[at], gx_sem, (q, d), device(z, p, c))
            for d, p in enumerate(x_peers)
        ])

    def stage_gx(q):
        arrive("gx", q)
        at = rows_at(q * rc + c * hr, hr)
        start("gc", q, [remote(sketch.at[at], sketch.at[at], gc_sem, (q,), core_peer)])

    def stage_gc(q):
        arrive("gc", q)
        at = pl.ds(q * rc, rc)
        block = sketch[at, :]
        turned = block.T
        gram = jnp.dot(turned, block, precision=HIGHEST, preferred_element_type=F32)
        gram_ref[...] = gram if q == 0 else gram_ref[...] + gram
        high = turned.astype(BF16)
        split[0:k, :] = high
        split[k:2 * k, :] = (turned - high.astype(F32)).astype(BF16)
        tile = 256

        @pl.loop(0, width // tile)
        def _(i):
            cols = pl.ds(pl.multiple_of(i * tile, tile), tile)
            both = jnp.dot(split[...], slab[at, cols], preferred_element_type=F32)
            cross = both[0:k] + both[k:2 * k]
            cross_ref[:, cols] = cross if q == 0 else cross_ref[:, cols] + cross

    stages = [stage_compute, stage_core, stage_x, stage_z, stage_gz, stage_gx, stage_gc]
    for t in range(nch + len(stages) - 1):
        for s in reversed(range(len(stages))):
            if 0 <= t - s < nch:
                stages[s](t - s)
    for copy in sent:
        copy.wait_send()


def factor_kernel(gram_ref, cross_ref, out_ref, work, inverse):
    k = gram_ref.shape[0]
    block, panel, lanes = 32, 8, 128
    work[:, 0:k] = gram_ref[...]
    row_at = lax.broadcasted_iota(jnp.int32, (k, k), 0)
    col_at = lax.broadcasted_iota(jnp.int32, (k, k), 1)
    work[:, k:2 * k] = (row_at == col_at).astype(F32)
    sub = lax.broadcasted_iota(jnp.int32, (block, lanes), 0)
    for b in range(k // block):
        first = b * block
        strips = [work[first:first + block, j * lanes:(j + 1) * lanes] for j in range(2 * k // lanes)]
        scale = jnp.zeros((block, lanes), F32)
        for p in range(block // panel):
            base = first + p * panel
            strip, lane = base // lanes, base % lanes
            columns = [
                jnp.broadcast_to(strips[strip][:, lane + i:lane + i + 1], (block, lanes)) for i in range(panel)
            ]
            for i in range(panel):
                r = p * panel + i
                pivot = columns[i][r:r + 1, :]
                scale = jnp.where(sub == r, lax.rsqrt(pivot), scale)
                if r + 1 == block:
                    continue
                lower = jnp.where(sub > r, columns[i] * (1.0 / pivot), 0.0)
                for j in range(i + 1, panel):
                    columns[j] = columns[j] - lower * columns[j][r:r + 1, :]
                strips = [s - lower * s[r:r + 1, :] for s in strips]
        done = jnp.concatenate([s * scale for s in strips], axis=1)
        inverse[first:first + block, :] = done[:, k:2 * k]
        if first + block < k:
            after = first + block
            update = lax.dot_general(
                done[:, after:k], done, (((0,), (0,)), ((), ())),
                precision=HIGHEST, preferred_element_type=F32,
            )
            work[after:k, :] = work[after:k, :] - update

    tile = 256

    @pl.loop(0, cross_ref.shape[1] // tile)
    def _(i):
        cols = pl.ds(pl.multiple_of(i * tile, tile), tile)
        out_ref[:, cols] = jnp.dot(
            inverse[...], cross_ref[:, cols], precision=HIGHEST, preferred_element_type=F32
        )


def local(ncol, slab, test):
    rows, width = slab.shape
    k = test.shape[1]
    chips = ncol // 2
    nx = 2 ** (chips.bit_length() // 3) if chips > 1 else 1
    nz = chips // nx
    nch = max(1, min(4, rows // (8 * ncol)))
    rc = rows // nch
    hr, xr, own = rc // 2, rc // (2 * nx), rc // ncol
    dma = pltpu.SemaphoreType.DMA
    gram, cross = pl.pallas_call(
        functools.partial(sketch_kernel, nx, nz, nch),
        out_shape=(jax.ShapeDtypeStruct((k, k), F32), jax.ShapeDtypeStruct((k, width), F32)),
        in_specs=[pl.BlockSpec(memory_space=pl.ANY)] * 2,
        out_specs=(pl.BlockSpec(memory_space=pltpu.VMEM),) * 2,
        scratch_shapes=[
            pltpu.VMEM((rows, width), BF16),
            pltpu.VMEM((width, k), BF16),
            pltpu.VMEM((rows, k), F32),
            pltpu.VMEM((nch, hr, k), F32),
            pltpu.VMEM((nch, hr, k), F32),
            pltpu.VMEM((nch, nx - 1, xr, k), F32),
            pltpu.VMEM((nch, xr, k), F32),
            pltpu.VMEM((nch, nz - 1, own, k), F32),
            pltpu.VMEM((rows, k), F32),
            pltpu.VMEM((2 * k, rc), BF16),
            dma((nch + 1,)),
            dma((2, nch)),
            dma((2, nch, nx - 1)),
            dma((2, nch, nz - 1)),
            dma((2, nch, nz - 1)),
            dma((2, nch, nx - 1)),
            dma((2, nch)),
        ],
        compiler_params=pltpu.CompilerParams(
            collective_id=0, has_side_effects=True, vmem_limit_bytes=48 * 2 ** 20
        ),
    )(slab, test)
    return pl.pallas_call(
        factor_kernel,
        out_shape=jax.ShapeDtypeStruct((k, width), F32),
        in_specs=[pl.BlockSpec(memory_space=pltpu.VMEM)] * 2,
        out_specs=pl.BlockSpec(memory_space=pltpu.VMEM),
        scratch_shapes=[pltpu.VMEM((k, 2 * k), F32), pltpu.VMEM((k, k), F32)],
        compiler_params=pltpu.CompilerParams(vmem_limit_bytes=32 * 2 ** 20),
    )(gram, cross)


def solution(mesh):
    return jax.shard_map(
        functools.partial(local, mesh.shape["col"]),
        mesh=mesh,
        in_specs=(P("groups", "col"), P("col", None)),
        out_specs=P("groups", "col"),
        check_vma=False,
    )
```

time: 206 us -> 66.1 us (0.32)
  waiting for transfers between devices: 101 us -> 0 us
  Pallas kernels: 0 us -> 64.7 us
  other arithmetic: 56.5 us -> 0 us
  matrix products: 26.1 us -> 0 us
  between operations: 14.8 us -> 0.01 us
  local copies, waits for them, and re-layouts: 8.03 us -> 1.22 us
    psum x1 -> x0, waiting for transfers between devices: 101 us -> none  [local(): sketch = lax.psum(partial_sketch, 'col')]
    pallas_call x0 -> x2, Pallas kernels: none -> 64.7 us  [the longest x1 51 us: local(): pl.pallas_call(functools.partial(sketch_kernel, nx, nz, nch), out_shape=(...]
    another operation x9 -> x0, other arithmetic: 55.5 us -> none  [the longest x6 34 us: orthonormal(): lower_factor = jnp.linalg.cholesky(gram_matrix)]
    dot_general x3 -> x0, matrix products: 19.8 us -> none  [the longest x1 7.06 us: contract_rows(): lax.dot_general(left, right, (((0,), (0,)), ((), ())), preferred_element_...]
    another operation x5 -> x0, matrix products: 6.26 us -> none  [the longest x3 3.96 us: orthonormal(): jax.scipy.linalg.solve_triangular(lower_factor, sketch_part.T, lower=True)]
    another operation x9 -> x0, local copies, waits for them, and re-layouts: 5.26 us -> none
  transfers between devices with their start and end apart: 1 -> 0, of which waited for: 1 -> 0; matrix products, arithmetic and copies ran while one was open for 0% -> 0% of each run, Pallas kernels for 0% -> 0%
where the time goes in v1:
time: 66.1 us; the launch traced here: 65.9 us
  Pallas kernels  64.7 us (98%)
  local copies, waits for them, and re-layouts  1.22 us (2%)
    pallas_call x1, Pallas kernels, local(): pl.pallas_call(functools.partial(sketch_kernel, nx, nz, nch), out_shape=(...  51 us
    pallas_call x1, Pallas kernels, local(): pl.pallas_call(factor_kernel, out_shape=jax.ShapeDtypeStruct((k, width),...  13.7 us

profile of v1, /device:TPU:0, one launch (start us, length us, event | category | flops | bytes accessed | tf_op | source)
XLA Modules:
  0.0 65.9 jit_solution(4216381646905992868)
XLA Ops:
  0.0 0.0 copy-start
  0.0 1.2 %copy-done = bf16[2048,256]{1,0:T(8,128)(2,1)S(1)} copy-done((bf16[2048,256]{1,0:T(8,128)(2,1)S(1)}, bf16[2048,256]{1,0:T(8,128)(2,1)}, u32[]{:S(2)}) %copy-start) | copy-done | bytes 1048600
  1.2 51.0 %shard_map.28 = (f32[256,256]{1,0:T(8,128)S(1)}, f32[256,2048]{1,0:T(8,128)S(1)}) custom-call(bf16[2048,2048]{1,0:T(8,128)(2,1)} %slab_hbm.1, bf16[2048,256]{1,0:T(8,128)(2,1)S(1)} %copy-done), custom_call_target="tpu_custom_call" | custom-call | tf_op jit(solution)/shard_map/pallas_call | solution.py:221
  52.2 13.7 %shard_map.29 = f32[256,2048]{1,0:T(8,128)} custom-call(f32[256,256]{1,0:T(8,128)S(1)} %get-tuple-element.7.gram_ref, f32[256,2048]{1,0:T(8,128)S(1)} %get-tuple-element.8.cross_ref), custom_call_target="tpu_custom_call" | custom-call | tf_op jit(solution)/shard_map/pallas_call | solution.py:249
Async XLA Ops:
  0.0 1.2 %copy-start = (bf16[2048,256]{1,0:T(8,128)(2,1)S(1)}, bf16[2048,256]{1,0:T(8,128)(2,1)}, u32[]{:S(2)}) copy-start(bf16[2048,256]{1,0:T(8,128)(2,1)} %test_hbm.1) | copy-start | bytes 3145732

commit v2 on v1

v2 whole, which is shorter than its diff:
```python
import functools

import jax
import jax.numpy as jnp
from jax import lax
from jax.experimental import pallas as pl
from jax.experimental.pallas import tpu as pltpu
from jax.sharding import PartitionSpec as P

F32 = jnp.float32
BF16 = jnp.bfloat16
MESH = pl.DeviceIdType.MESH
HIGHEST = lax.Precision.HIGHEST


def factor(gram_ref, inverse, work, steps):
    k = gram_ref.shape[0]
    block, panel, lanes = 32, 8, 128
    work[:, 0:k] = gram_ref[...]
    row_at = lax.broadcasted_iota(jnp.int32, (k, k), 0)
    col_at = lax.broadcasted_iota(jnp.int32, (k, k), 1)
    work[:, k:2 * k] = (row_at == col_at).astype(F32)
    sub = lax.broadcasted_iota(jnp.int32, (block, lanes), 0)
    plan = {1: 1, 3: 2, 4: 1, 5: 2, 6: 1, 7: 1}
    for b in range(k // block):
        for _ in range(plan.get(b, 0)):
            if steps:
                steps.pop(0)()
        first = b * block
        strips = [work[first:first + block, j * lanes:(j + 1) * lanes] for j in range(2 * k // lanes)]
        scale = jnp.zeros((block, lanes), F32)
        for p in range(block // panel):
            base = first + p * panel
            strip, lane = base // lanes, base % lanes
            columns = [
                jnp.broadcast_to(strips[strip][:, lane + i:lane + i + 1], (block, lanes)) for i in range(panel)
            ]
            for i in range(panel):
                r = p * panel + i
                pivot = columns[i][r:r + 1, :]
                scale = jnp.where(sub == r, lax.rsqrt(pivot), scale)
                if r + 1 == block:
                    continue
                lower = jnp.where(sub > r, columns[i] * (1.0 / pivot), 0.0)
                for j in range(i + 1, panel):
                    columns[j] = columns[j] - lower * columns[j][r:r + 1, :]
                strips = [s - lower * s[r:r + 1, :] for s in strips]
        done = jnp.concatenate([s * scale for s in strips], axis=1)
        inverse[first:first + block, :] = done[:, k:2 * k]
        if first + block < k:
            after = first + block
            update = lax.dot_general(
                done[:, after:k], done, (((0,), (0,)), ((), ())),
                precision=HIGHEST, preferred_element_type=F32,
            )
            work[after:k, :] = work[after:k, :] - update
    return steps


def project_kernel(inverse_ref, cross_ref, out_ref):
    out_ref[...] = jnp.dot(
        inverse_ref[...], cross_ref[...], precision=HIGHEST, preferred_element_type=F32
    )


def sketch_kernel(
    nx, nz, nch, slab_hbm, test_hbm, inverse_ref, cross_ref,
    slab, test, part, core_in, half, x_in, quarter, z_in, sketch, split,
    gram_own, gram_c_in, gram_c, gram_x_in, gram_x, gram_z_in, gram, work,
    load_sem, core_sem, x_sem, z_sem, gz_sem, gx_sem, gc_sem,
    rc_sem, rx_sem, rz_sem, bz_sem, bx_sem, bc_sem,
):
    ncol = 2 * nx * nz
    rows, width = slab.shape
    k = test.shape[1]
    rc = rows // nch
    hr, xr, own = rc // 2, rc // (2 * nx), rc // ncol
    me = lax.axis_index("col")
    c = lax.rem(me, 2)
    x = lax.rem(me // 2, nx)
    z = me // (2 * nx)

    def device(z_, x_, c_):
        return {"col": (z_ * nx + x_) * 2 + c_}

    core_peer = device(z, x, 1 - c)
    x_peers = [lax.rem(x + d, nx) for d in range(1, nx)]
    z_peers = [lax.rem(z + d, nz) for d in range(1, nz)]

    load_test = pltpu.make_async_copy(test_hbm, test, load_sem.at[nch])
    load_test.start()
    loads = []
    for q in range(nch):
        at = pl.ds(q * rc, rc)
        load = pltpu.make_async_copy(slab_hbm.at[at], slab.at[at], load_sem.at[q])
        load.start()
        loads.append(load)

    barrier = pltpu.get_barrier_semaphore()
    peers = [core_peer] + [device(z, p, c) for p in x_peers] + [device(p, x, c) for p in z_peers]
    for peer in peers:
        pl.semaphore_signal(barrier, inc=1, device_id=peer, device_id_type=MESH)

    def remote(src, dst, sems, index, peer):
        return pltpu.make_async_remote_copy(
            src_ref=src, dst_ref=dst,
            send_sem=sems.at[(0,) + index], recv_sem=sems.at[(1,) + index],
            device_id=peer, device_id_type=MESH,
        )

    sent = []
    flights = {}

    def start(name, q, copies):
        for copy in copies:
            copy.start()
        sent.extend(copies)
        flights[name, q] = copies

    def arrive(name, q):
        for copy in flights[name, q]:
            copy.wait_recv()

    def rows_at(first, size):
        return pl.ds(pl.multiple_of(first, 8), size)

    def stage_compute(q):
        if q == 0:
            load_test.wait()
        loads[q].wait()
        tile = 256

        @pl.loop(0, rc // tile)
        def _(i):
            at = rows_at(q * rc + i * tile, tile)
            part[at, :] = jnp.dot(slab[at, :], test[...], preferred_element_type=F32)

        if q == 0:
            pl.semaphore_wait(barrier, len(peers))
        src = part.at[rows_at(q * rc + (1 - c) * hr, hr)]
        start("core", q, [remote(src, core_in.at[q], core_sem, (q,), core_peer)])

    def stage_core(q):
        arrive("core", q)
        half[q] = part[rows_at(q * rc + c * hr, hr), :] + core_in[q]
        start("x", q, [
            remote(half.at[q, rows_at(p * xr, xr)], x_in.at[q, d], x_sem, (q, d), device(z, p, c))
            for d, p in enumerate(x_peers)
        ])

    def stage_x(q):
        arrive("x", q)
        total = half[q, rows_at(x * xr, xr), :]
        for d in range(nx - 1):
            total = total + x_in[q, d]
        quarter[q] = total
        start("z", q, [
            remote(quarter.at[q, rows_at(p * own, own)], z_in.at[q, d], z_sem, (q, d), device(p, x, c))
            for d, p in enumerate(z_peers)
        ])

    def stage_z(q):
        arrive("z", q)
        total = quarter[q, rows_at(z * own, own), :]
        for d in range(nz - 1):
            total = total + z_in[q, d]
        at = rows_at(q * rc + c * hr + x * xr + z * own, own)
        sketch[at, :] = total
        square = lax.dot_general(
            total, total, (((0,), (0,)), ((), ())), precision=HIGHEST, preferred_element_type=F32
        )
        gram_own[...] = square if q == 0 else gram_own[...] + square

    def gather_z(q):
        at = rows_at(q * rc + c * hr + x * xr + z * own, own)
        start("gz", q, [
            remote(sketch.at[at], sketch.at[at], gz_sem, (q, d), device(p, x, c))
            for d, p in enumerate(z_peers)
        ])

    def gather_x(q):
        arrive("gz", q)
        at = rows_at(q * rc + c * hr + x * xr, xr)
        start("gx", q, [
            remote(sketch.at[at], sketch.at[at], gx_sem, (q, d), device(z, p, c))
            for d, p in enumerate(x_peers)
        ])

    def gather_core(q):
        arrive("gx", q)
        at = rows_at(q * rc + c * hr, hr)
        start("gc", q, [remote(sketch.at[at], sketch.at[at], gc_sem, (q,), core_peer)])

    def cross(q):
        arrive("gc", q)
        at = pl.ds(q * rc, rc)
        block = sketch[at, :]
        turned = block.T
        high = turned.astype(BF16)
        split[0:k, :] = high
        split[k:2 * k, :] = (turned - high.astype(F32)).astype(BF16)
        tile = 256

        @pl.loop(0, width // tile)
        def _(i):
            cols = pl.ds(pl.multiple_of(i * tile, tile), tile)
            both = jnp.dot(split[...], slab[at, cols], preferred_element_type=F32)
            term = both[0:k] + both[k:2 * k]
            cross_ref[:, cols] = term if q == 0 else cross_ref[:, cols] + term

    stages = [stage_compute, stage_core, stage_x, stage_z]
    for t in range(nch + len(stages) - 1):
        for s in reversed(range(len(stages))):
            if 0 <= t - s < nch:
                stages[s](t - s)

    kc, kx, kz = k // 2, k // (2 * nx), k // ncol
    start("rc", 0, [remote(gram_own.at[rows_at((1 - c) * kc, kc)], gram_c_in, rc_sem, (0,), core_peer)])
    arrive("rc", 0)
    gram_c[...] = gram_own[rows_at(c * kc, kc), :] + gram_c_in[...]
    start("rx", 0, [
        remote(gram_c.at[rows_at(p * kx, kx)], gram_x_in.at[d], rx_sem, (d,), device(z, p, c))
        for d, p in enumerate(x_peers)
    ])
    arrive("rx", 0)
    total = gram_c[rows_at(x * kx, kx), :]
    for d in range(nx - 1):
        total = total + gram_x_in[d]
    gram_x[...] = total
    spread = kz >= 8
    start("rz", 0, [
        remote(gram_x.at[rows_at(p * kz, kz)] if spread else gram_x, gram_z_in.at[d], rz_sem, (d,), device(p, x, c))
        for d, p in enumerate(z_peers)
    ])
    arrive("rz", 0)
    total = gram_x[rows_at(z * kz, kz), :] if spread else total
    for d in range(nz - 1):
        total = total + gram_z_in[d]
    if spread:
        at = rows_at(c * kc + x * kx + z * kz, kz)
        gram[at, :] = total
        start("bz", 0, [
            remote(gram.at[at], gram.at[at], bz_sem, (d,), device(p, x, c)) for d, p in enumerate(z_peers)
        ])
        gather_z(0)
        arrive("bz", 0)
    else:
        gram[rows_at(c * kc + x * kx, kx), :] = total
        gather_z(0)
    at = rows_at(c * kc + x * kx, kx)
    start("bx", 0, [
        remote(gram.at[at], gram.at[at], bx_sem, (d,), device(z, p, c)) for d, p in enumerate(x_peers)
    ])
    for q in range(1, nch):
        gather_z(q)
    arrive("bx", 0)
    at = rows_at(c * kc, kc)
    start("bc", 0, [remote(gram.at[at], gram.at[at], bc_sem, (0,), core_peer)])
    arrive("bc", 0)

    steps = []
    for t in range(nch + 2):
        if t < nch:
            steps.append(functools.partial(gather_x, t))
        if 1 <= t <= nch:
            steps.append(functools.partial(gather_core, t - 1))
        if t >= 2:
            steps.append(functools.partial(cross, t - 2))
    left = factor(gram, inverse_ref, work, steps)
    for step in left:
        step()
    for copy in sent:
        copy.wait_send()


def local(ncol, slab, test):
    rows, width = slab.shape
    k = test.shape[1]
    chips = ncol // 2
    nx = 2 ** (chips.bit_length() // 3) if chips > 1 else 1
    nz = chips // nx
    nch = max(1, min(4, rows // (8 * ncol)))
    rc = rows // nch
    hr, xr, own = rc // 2, rc // (2 * nx), rc // ncol
    dma = pltpu.SemaphoreType.DMA
    kc, kx, kz = k // 2, k // (2 * nx), k // ncol
    inverse, cross = pl.pallas_call(
        functools.partial(sketch_kernel, nx, nz, nch),
        out_shape=(jax.ShapeDtypeStruct((k, k), F32), jax.ShapeDtypeStruct((k, width), F32)),
        in_specs=[pl.BlockSpec(memory_space=pltpu.HBM)] * 2,
        out_specs=(pl.BlockSpec(memory_space=pltpu.VMEM),) * 2,
        scratch_shapes=[
            pltpu.VMEM((rows, width), BF16),
            pltpu.VMEM((width, k), BF16),
            pltpu.VMEM((rows, k), F32),
            pltpu.VMEM((nch, hr, k), F32),
            pltpu.VMEM((nch, hr, k), F32),
            pltpu.VMEM((nch, nx - 1, xr, k), F32),
            pltpu.VMEM((nch, xr, k), F32),
            pltpu.VMEM((nch, nz - 1, own, k), F32),
            pltpu.VMEM((rows, k), F32),
            pltpu.VMEM((2 * k, rc), BF16),
            pltpu.VMEM((k, k), F32),
            pltpu.VMEM((kc, k), F32),
            pltpu.VMEM((kc, k), F32),
            pltpu.VMEM((nx - 1, kx, k), F32),
            pltpu.VMEM((kx, k), F32),
            pltpu.VMEM((nz - 1, kz if kz >= 8 else kx, k), F32),
            pltpu.VMEM((k, k), F32),
            pltpu.VMEM((k, 2 * k), F32),
            dma((nch + 1,)),
            dma((2, nch)),
            dma((2, nch, nx - 1)),
            dma((2, nch, nz - 1)),
            dma((2, nch, nz - 1)),
            dma((2, nch, nx - 1)),
            dma((2, nch)),
            dma((2, 1)),
            dma((2, nx - 1)),
            dma((2, nz - 1)),
            dma((2, nz - 1)),
            dma((2, nx - 1)),
            dma((2, 1)),
        ],
        compiler_params=pltpu.CompilerParams(
            collective_id=0, has_side_effects=True, vmem_limit_bytes=48 * 2 ** 20
        ),
    )(slab, test)
    tile = 512
    return pl.pallas_call(
        project_kernel,
        grid=(width // tile,),
        out_shape=jax.ShapeDtypeStruct((k, width), F32),
        in_specs=[
            pl.BlockSpec((k, k), lambda i: (0, 0)),
            pl.BlockSpec((k, tile), lambda i: (0, i)),
        ],
        out_specs=pl.BlockSpec((k, tile), lambda i: (0, i)),
        compiler_params=pltpu.CompilerParams(vmem_limit_bytes=24 * 2 ** 20),
    )(inverse, cross)


def solution(mesh):
    return jax.shard_map(
        functools.partial(local, mesh.shape["col"]),
        mesh=mesh,
        in_specs=(P("groups", "col"), P("col", None)),
        out_specs=P("groups", "col"),
        check_vma=False,
    )
```

time: 66.1 us -> 75.5 us (1.14)
  Pallas kernels: 64.7 us -> 74.1 us
    pallas_call x1, Pallas kernels: 51 us -> 70.5 us  [local(): pl.pallas_call(functools.partial(sketch_kernel, nx, nz, nch), out_shape=(...]
    pallas_call x1, Pallas kernels: 13.7 us -> 3.57 us  [local(): pl.pallas_call(project_kernel, grid=(width // tile,), out_shape=jax.Shape...]
where the time goes in v2:
time: 75.5 us; the launch traced here: 75.4 us
  Pallas kernels  74.1 us (98%)
  local copies, waits for them, and re-layouts  1.22 us (2%)
    pallas_call x1, Pallas kernels, local(): pl.pallas_call(functools.partial(sketch_kernel, nx, nz, nch), out_shape=(...  70.5 us
    pallas_call x1, Pallas kernels, local(): pl.pallas_call(project_kernel, grid=(width // tile,), out_shape=jax.Shape...  3.57 us

profile of v2, /device:TPU:0, one launch (start us, length us, event | category | flops | bytes accessed | tf_op | source)
XLA Modules:
  0.0 75.4 jit_solution(9339336709330457259)
XLA Ops:
  0.0 0.0 copy-start
  0.0 1.2 %copy-done = bf16[2048,256]{1,0:T(8,128)(2,1)S(1)} copy-done((bf16[2048,256]{1,0:T(8,128)(2,1)S(1)}, bf16[2048,256]{1,0:T(8,128)(2,1)}, u32[]{:S(2)}) %copy-start) | copy-done | bytes 1048600
  1.2 70.5 %shard_map.28 = (f32[256,256]{1,0:T(8,128)S(1)}, f32[256,2048]{1,0:T(8,128)S(1)}) custom-call(bf16[2048,2048]{1,0:T(8,128)(2,1)} %slab_hbm.1, bf16[2048,256]{1,0:T(8,128)(2,1)S(1)} %copy-done), custom_call_target="tpu_custom_call" | custom-call | tf_op jit(solution)/shard_map/pallas_call | solution.py:287
  71.8 3.6 %shard_map.29 = f32[256,2048]{1,0:T(8,128)} custom-call(f32[256,256]{1,0:T(8,128)S(1)} %get-tuple-element.7.inverse_ref, f32[256,2048]{1,0:T(8,128)S(1)} %get-tuple-element.8.cross_ref), custom_call_target="tpu_custom_call" | custom-call | tf_op jit(solution)/shard_map/pallas_call | solution.py:330
Async XLA Ops:
  0.0 1.2 %copy-start = (bf16[2048,256]{1,0:T(8,128)(2,1)S(1)}, bf16[2048,256]{1,0:T(8,128)(2,1)}, u32[]{:S(2)}) copy-start(bf16[2048,256]{1,0:T(8,128)(2,1)} %test_hbm.1) | copy-start | bytes 3145732

commit v3 on v1

--- a/solution.py
+++ b/solution.py
@@ -76,7 +76,7 @@
         if q == 0:
             load_test.wait()
         loads[q].wait()
-        tile = 128
+        tile = 256
 
         @pl.loop(0, rc // tile)
         def _(i):
@@ -152,15 +152,15 @@
             cross_ref[:, cols] = cross if q == 0 else cross_ref[:, cols] + cross
 
     stages = [stage_compute, stage_core, stage_x, stage_z, stage_gz, stage_gx, stage_gc]
-    for t in range(nch + len(stages) - 1):
-        for s in reversed(range(len(stages))):
-            if 0 <= t - s < nch:
-                stages[s](t - s)
+    begin = [0, 2, 5, 8, 11, 13, 15]
+    order = sorted((q + begin[s], -s, q) for s in range(len(stages)) for q in range(nch))
+    for _, s, q in order:
+        stages[-s](q)
     for copy in sent:
         copy.wait_send()
 
 
-def factor_kernel(gram_ref, cross_ref, out_ref, work, inverse):
+def factor_kernel(gram_ref, cross_ref, out_ref, work, inverse, split):
     k = gram_ref.shape[0]
     block, panel, lanes = 32, 8, 128
     work[:, 0:k] = gram_ref[...]
@@ -198,14 +198,20 @@
             )
             work[after:k, :] = work[after:k, :] - update
 
+    high = inverse[...].astype(BF16)
+    split[0:k, :] = high
+    split[k:2 * k, :] = (inverse[...] - high.astype(F32)).astype(BF16)
     tile = 256
 
     @pl.loop(0, cross_ref.shape[1] // tile)
     def _(i):
         cols = pl.ds(pl.multiple_of(i * tile, tile), tile)
-        out_ref[:, cols] = jnp.dot(
-            inverse[...], cross_ref[:, cols], precision=HIGHEST, preferred_element_type=F32
-        )
+        term = cross_ref[:, cols]
+        term_high = term.astype(BF16)
+        term_low = (term - term_high.astype(F32)).astype(BF16)
+        both = jnp.dot(split[...], term_high, preferred_element_type=F32)
+        rest = jnp.dot(split[0:k, :], term_low, preferred_element_type=F32)
+        out_ref[:, cols] = both[0:k] + (both[k:2 * k] + rest)
 
 
 def local(ncol, slab, test):
@@ -214,7 +220,7 @@
     chips = ncol // 2
     nx = 2 ** (chips.bit_length() // 3) if chips > 1 else 1
     nz = chips // nx
-    nch = max(1, min(4, rows // (8 * ncol)))
+    nch = max(1, min(8, rows // (8 * ncol)))
     rc = rows // nch
     hr, xr, own = rc // 2, rc // (2 * nx), rc // ncol
     dma = pltpu.SemaphoreType.DMA
@@ -251,7 +257,7 @@
         out_shape=jax.ShapeDtypeStruct((k, width), F32),
         in_specs=[pl.BlockSpec(memory_space=pltpu.VMEM)] * 2,
         out_specs=pl.BlockSpec(memory_space=pltpu.VMEM),
-        scratch_shapes=[pltpu.VMEM((k, 2 * k), F32), pltpu.VMEM((k, k), F32)],
+        scratch_shapes=[pltpu.VMEM((k, 2 * k), F32), pltpu.VMEM((k, k), F32), pltpu.VMEM((2 * k, k), BF16)],
         compiler_params=pltpu.CompilerParams(vmem_limit_bytes=32 * 2 ** 20),
     )(gram, cross)
 

time: 66.1 us -> 63 us (0.953)
  Pallas kernels: 64.7 us -> 61.6 us
    pallas_call x1, Pallas kernels: 51 us -> 48.8 us  [local(): pl.pallas_call(functools.partial(sketch_kernel, nx, nz, nch), out_shape=(...]
    pallas_call x1, Pallas kernels: 13.7 us -> 12.8 us  [local(): pl.pallas_call(factor_kernel, out_shape=jax.ShapeDtypeStruct((k, width),...]
where the time goes in v3:
time: 63 us; the launch traced here: 62.9 us
  Pallas kernels  61.6 us (98%)
  local copies, waits for them, and re-layouts  1.22 us (2%)
    pallas_call x1, Pallas kernels, local(): pl.pallas_call(functools.partial(sketch_kernel, nx, nz, nch), out_shape=(...  48.8 us
    pallas_call x1, Pallas kernels, local(): pl.pallas_call(factor_kernel, out_shape=jax.ShapeDtypeStruct((k, width),...  12.8 us

profile of v3, /device:TPU:0, one launch (start us, length us, event | category | flops | bytes accessed | tf_op | source)
XLA Modules:
  0.0 62.9 jit_solution(15199352714221241544)
XLA Ops:
  0.0 0.0 copy-start
  0.0 1.2 %copy-done = bf16[2048,256]{1,0:T(8,128)(2,1)S(1)} copy-done((bf16[2048,256]{1,0:T(8,128)(2,1)S(1)}, bf16[2048,256]{1,0:T(8,128)(2,1)}, u32[]{:S(2)}) %copy-start) | copy-done | bytes 1048600
  1.2 48.8 %shard_map.28 = (f32[256,256]{1,0:T(8,128)S(1)}, f32[256,2048]{1,0:T(8,128)S(1)}) custom-call(bf16[2048,2048]{1,0:T(8,128)(2,1)} %slab_hbm.1, bf16[2048,256]{1,0:T(8,128)(2,1)S(1)} %copy-done), custom_call_target="tpu_custom_call" | custom-call | tf_op jit(solution)/shard_map/pallas_call | solution.py:227
  50.1 12.8 %shard_map.29 = f32[256,2048]{1,0:T(8,128)} custom-call(f32[256,256]{1,0:T(8,128)S(1)} %get-tuple-element.7.gram_ref, f32[256,2048]{1,0:T(8,128)S(1)} %get-tuple-element.8.cross_ref), custom_call_target="tpu_custom_call" | custom-call | tf_op jit(solution)/shard_map/pallas_call | solution.py:255
Async XLA Ops:
  0.0 1.2 %copy-start = (bf16[2048,256]{1,0:T(8,128)(2,1)S(1)}, bf16[2048,256]{1,0:T(8,128)(2,1)}, u32[]{:S(2)}) copy-start(bf16[2048,256]{1,0:T(8,128)(2,1)} %test_hbm.1) | copy-start | bytes 3145732

commit v4 on v3

--- a/solution.py
+++ b/solution.py
@@ -170,11 +170,13 @@
     sub = lax.broadcasted_iota(jnp.int32, (block, lanes), 0)
     for b in range(k // block):
         first = b * block
-        strips = [work[first:first + block, j * lanes:(j + 1) * lanes] for j in range(2 * k // lanes)]
+        low = first // lanes
+        left, right = low * lanes, k + (low + 1) * lanes
+        strips = [work[first:first + block, j:j + lanes] for j in range(left, right, lanes)]
         scale = jnp.zeros((block, lanes), F32)
         for p in range(block // panel):
             base = first + p * panel
-            strip, lane = base // lanes, base % lanes
+            strip, lane = base // lanes - low, base % lanes
             columns = [
                 jnp.broadcast_to(strips[strip][:, lane + i:lane + i + 1], (block, lanes)) for i in range(panel)
             ]
@@ -189,14 +191,16 @@
                     columns[j] = columns[j] - lower * columns[j][r:r + 1, :]
                 strips = [s - lower * s[r:r + 1, :] for s in strips]
         done = jnp.concatenate([s * scale for s in strips], axis=1)
-        inverse[first:first + block, :] = done[:, k:2 * k]
+        inverse[first:first + block, 0:right - k] = done[:, k - left:]
+        if right < 2 * k:
+            inverse[first:first + block, right - k:] = jnp.zeros((block, 2 * k - right), F32)
         if first + block < k:
             after = first + block
             update = lax.dot_general(
-                done[:, after:k], done, (((0,), (0,)), ((), ())),
+                done[:, after - left:k - left], done, (((0,), (0,)), ((), ())),
                 precision=HIGHEST, preferred_element_type=F32,
             )
-            work[after:k, :] = work[after:k, :] - update
+            work[after:k, left:right] = work[after:k, left:right] - update
 
     high = inverse[...].astype(BF16)
     split[0:k, :] = high

time: 63 us -> 62.9 us (level)
  no operation moved by 1% of the time
where the time goes in v4:
time: 62.9 us; the launch traced here: 62.8 us
  Pallas kernels  61.5 us (98%)
  local copies, waits for them, and re-layouts  1.22 us (2%)
    pallas_call x1, Pallas kernels, local(): pl.pallas_call(functools.partial(sketch_kernel, nx, nz, nch), out_shape=(...  48.8 us
    pallas_call x1, Pallas kernels, local(): pl.pallas_call(factor_kernel, out_shape=jax.ShapeDtypeStruct((k, width),...  12.7 us

profile of v4, /device:TPU:0, one launch (start us, length us, event | category | flops | bytes accessed | tf_op | source)
XLA Modules:
  0.0 62.8 jit_solution(17730786830233327951)
XLA Ops:
  0.0 0.0 copy-start
  0.0 1.2 %copy-done = bf16[2048,256]{1,0:T(8,128)(2,1)S(1)} copy-done((bf16[2048,256]{1,0:T(8,128)(2,1)S(1)}, bf16[2048,256]{1,0:T(8,128)(2,1)}, u32[]{:S(2)}) %copy-start) | copy-done | bytes 1048600
  1.2 48.8 %shard_map.28 = (f32[256,256]{1,0:T(8,128)S(1)}, f32[256,2048]{1,0:T(8,128)S(1)}) custom-call(bf16[2048,2048]{1,0:T(8,128)(2,1)} %slab_hbm.1, bf16[2048,256]{1,0:T(8,128)(2,1)S(1)} %copy-done), custom_call_target="tpu_custom_call" | custom-call | tf_op jit(solution)/shard_map/pallas_call | solution.py:231
  50.1 12.7 %shard_map.29 = f32[256,2048]{1,0:T(8,128)} custom-call(f32[256,256]{1,0:T(8,128)S(1)} %get-tuple-element.7.gram_ref, f32[256,2048]{1,0:T(8,128)S(1)} %get-tuple-element.8.cross_ref), custom_call_target="tpu_custom_call" | custom-call | tf_op jit(solution)/shard_map/pallas_call | solution.py:259
Async XLA Ops:
  0.0 1.2 %copy-start = (bf16[2048,256]{1,0:T(8,128)(2,1)S(1)}, bf16[2048,256]{1,0:T(8,128)(2,1)}, u32[]{:S(2)}) copy-start(bf16[2048,256]{1,0:T(8,128)(2,1)} %test_hbm.1) | copy-start | bytes 3145732
